TPU v7x, 1024 devices: a whole 8x8x8 slice. The times are simulated.
1024 devices in a mesh: band: 16 (over x, core), dom: 64 (over z, y).
Axes of the slice: x: 8, y: 8, z: 8, core: 2. Of those that a mesh axis runs over, the one named last changes fastest.
Arguments:
- grid_latent: bfloat16 [262144, 512], P(('band', 'dom')), may hold values from -6 to 6
- mesh_latent: bfloat16 [32768, 512], P(('band', 'dom')), may hold values from -6 to 6
- send_rows: int32 [65536, 16], P(('band', 'dom')), may hold values from 0 to 255, as said below
- send_count: int32 [65536], P(('band', 'dom')), may hold values from 1 to 16, as said below
- enc_sender: int32 [524288], P(('band', 'dom')), may hold values from 0 to 1023, as said below
- enc_receiver: int32 [524288], P(('band', 'dom')), may hold values from 0 to 31, as said below
- move_to: int32 [32768], P(('band', 'dom')), may hold values from 0 to 511, as said below
- proc_sender: int32 [524288], P(('band', 'dom')), may hold values from 0 to 31
- proc_receiver: int32 [524288], P(('band', 'dom')), may hold values from 0 to 31
- enc_edge_w1: bfloat16 [1024, 512], replicated, may hold values from -0.1875 to 0.1875
- enc_edge_b1: float32 [512], replicated, may hold values from -3 to 3
- enc_edge_w2: bfloat16 [512, 512], replicated, may hold values from -0.25 to 0.25
- enc_edge_b2: float32 [512], replicated, may hold values from -2 to 2
- enc_node_w1: bfloat16 [1024, 512], replicated, may hold values from -0.1875 to 0.1875
- enc_node_b1: float32 [512], replicated, may hold values from -3 to 3
- enc_node_w2: bfloat16 [512, 512], replicated, may hold values from -0.25 to 0.25
- enc_node_b2: float32 [512], replicated, may hold values from -3 to 3
- enc_gain: float32 [512], replicated, may hold values from 0.1 to 1.9
- proc_edge_w1: bfloat16 [1024, 512], replicated, may hold values from -0.1875 to 0.1875
- proc_edge_b1: float32 [512], replicated, may hold values from -3 to 3
- proc_edge_w2: bfloat16 [512, 512], replicated, may hold values from -0.25 to 0.25
- proc_edge_b2: float32 [512], replicated, may hold values from -2 to 2
- proc_node_w1: bfloat16 [1024, 512], replicated, may hold values from -0.1875 to 0.1875
- proc_node_b1: float32 [512], replicated, may hold values from -3 to 3
- proc_node_w2: bfloat16 [512, 512], replicated, may hold values from -0.25 to 0.25
- proc_node_b2: float32 [512], replicated, may hold values from -3 to 3
- proc_gain: float32 [512], replicated, may hold values from 0.1 to 1.9
Outputs:
- mesh_out: bfloat16 [32768, 512], P(('band', 'dom'))
Inputs may be any that keep to these rules, and one draw needn't show every extreme that they name: `send_rows`: entries of a sender's list at or past the matching send_count are unused. `send_count`: in every band group one receiving dom index gets 16 rows from every sender. `enc_sender`: each value is s * 16 + k for a sender dom index s and k below the count that s sends to this device. `enc_receiver`: Non-decreasing within each device's 512 edges. `move_to`: value c * 32 + r: the row goes to row r of the device with band index c and the same dom index; a device sends at most 8 rows to other band indices, exactly 8 for some device; within each dom index the values form a permutation.
All inputs are finite; a program needn't handle non-finite values.
Results may differ from a plain program's by a relative error of at most 0.01.
Values may be sent and summed in bfloat16 or wider, within the bound.
A program may use at most 32 MiB of HBM per device.

v0:
```python
import jax
import jax.numpy as jnp
from jax import lax
from jax.sharding import PartitionSpec as P


def node_update(mesh, agg, node_w1, node_b1, node_w2, node_b2, gain):
    width = mesh.shape[1]
    agg_round = agg.astype(jnp.bfloat16)
    pre = jnp.dot(mesh, node_w1[:width], preferred_element_type=jnp.float32)
    pre = pre + jnp.dot(agg_round, node_w1[width:], preferred_element_type=jnp.float32) + node_b1
    hidden = jax.nn.silu(pre).astype(jnp.bfloat16)
    update = jnp.dot(hidden, node_w2, preferred_element_type=jnp.float32) + node_b2
    center = update - jnp.mean(update, axis=-1, keepdims=True)
    spread = jnp.mean(center * center, axis=-1, keepdims=True)
    normed = center * lax.rsqrt(spread + 1e-05)
    return (mesh.astype(jnp.float32) + gain * normed).astype(jnp.bfloat16)


def edge_sum(send_proj, recv_proj, sender, receiver, bias_one, weight_two, bias_two, count_rows):
    pre = jnp.take(send_proj, sender, axis=0) + jnp.take(recv_proj, receiver, axis=0) + bias_one
    hidden = jax.nn.silu(pre).astype(jnp.bfloat16)
    message = (jnp.dot(hidden, weight_two, preferred_element_type=jnp.float32) + bias_two).astype(
        jnp.bfloat16
    )
    one_hot = (receiver[:, None] == jnp.arange(count_rows)[None, :]).astype(jnp.bfloat16)
    return jnp.einsum("em,ed->md", one_hot, message, preferred_element_type=jnp.float32)


def shards(
    grid_latent,
    mesh_latent,
    send_rows,
    send_count,
    enc_sender,
    enc_receiver,
    move_to,
    proc_sender,
    proc_receiver,
    enc_edge_w1,
    enc_edge_b1,
    enc_edge_w2,
    enc_edge_b2,
    enc_node_w1,
    enc_node_b1,
    enc_node_w2,
    enc_node_b2,
    enc_gain,
    proc_edge_w1,
    proc_edge_b1,
    proc_edge_w2,
    proc_edge_b2,
    proc_node_w1,
    proc_node_b1,
    proc_node_w2,
    proc_node_b2,
    proc_gain,
):
    width = mesh_latent.shape[1]
    rows_here = mesh_latent.shape[0]
    peers, slots_each = send_rows.shape
    picked = jnp.take(grid_latent, send_rows.reshape(-1), axis=0).reshape(peers, slots_each, width)
    keep = jnp.arange(slots_each)[None, :] < send_count[:, None]
    picked = jnp.where(keep[:, :, None], picked, jnp.zeros_like(picked))
    w_sender = enc_edge_w1[:width]
    send_proj = jnp.einsum(
        "psd,dh->psh",
        lax.all_to_all(picked, "dom", split_axis=0, concat_axis=0, tiled=True),
        w_sender,
        preferred_element_type=jnp.float32,
    )
    send_proj = send_proj.reshape(peers * slots_each, -1)
    recv_proj = jnp.dot(mesh_latent, enc_edge_w1[width:], preferred_element_type=jnp.float32)
    enc_agg = edge_sum(
        send_proj,
        recv_proj,
        enc_sender,
        enc_receiver,
        enc_edge_b1,
        enc_edge_w2,
        enc_edge_b2,
        rows_here,
    )
    mesh_enc = node_update(
        mesh_latent, enc_agg, enc_node_w1, enc_node_b1, enc_node_w2, enc_node_b2, enc_gain
    )
    bands = lax.axis_size("band")
    dest_band = move_to // rows_here
    dest_slot = move_to % rows_here
    buckets = (
        jnp.zeros((bands, rows_here, width), jnp.bfloat16).at[dest_band, dest_slot].set(mesh_enc)
    )
    arrived = lax.all_to_all(buckets, "band", split_axis=0, concat_axis=0, tiled=True)
    proc_in = jnp.sum(arrived.astype(jnp.float32), axis=0).astype(jnp.bfloat16)
    psend_proj = jnp.dot(proc_in, proc_edge_w1[:width], preferred_element_type=jnp.float32)
    precv_proj = jnp.dot(proc_in, proc_edge_w1[width:], preferred_element_type=jnp.float32)
    proc_agg = edge_sum(
        psend_proj,
        precv_proj,
        proc_sender,
        proc_receiver,
        proc_edge_b1,
        proc_edge_w2,
        proc_edge_b2,
        rows_here,
    )
    return node_update(
        proc_in, proc_agg, proc_node_w1, proc_node_b1, proc_node_w2, proc_node_b2, proc_gain
    )


def solution(mesh):
    return jax.shard_map(
        shards,
        mesh=mesh,
        in_specs=(
            P(("band", "dom"), None),
            P(("band", "dom"), None),
            P(("band", "dom"), None),
            P(("band", "dom")),
            P(("band", "dom")),
            P(("band", "dom")),
            P(("band", "dom")),
            P(("band", "dom")),
            P(("band", "dom")),
            P(),
            P(),
            P(),
            P(),
            P(),
            P(),
            P(),
            P(),
            P(),
            P(),
            P(),
            P(),
            P(),
            P(),
            P(),
            P(),
            P(),
            P(),
        ),
        out_specs=P(("band", "dom"), None),
        check_vma=False,
    )
```

profile of v0, /device:TPU:1, one launch (start us, length us, event | category | flops | bytes accessed | tf_op | source)
XLA Modules:
  0.0 111.5 jit_solution(7547314956218926172)
XLA Ops:
  0.0 0.8 copy.32
  0.8 0.7 compare_and_fusion
  1.5 0.1 reshape.113
  1.7 0.1 copy.31
  1.8 0.7 iota_compare_fusion.4
  2.5 5.0 %gather_fusion = bf16[1024,512]{1,0:T(8,128)(2,1)S(1)} fusion(bf16[256,512]{1,0:T(8,128)(2,1)} %param.29, s32[1024]{0:T(1024)S(1)} %broadcast_clamp_fusion), kind=kCustom, calls=%fused_computation.3 | custom fusion | bytes 2101248 | tf_op jit(solution)/shard_map/jit(_take)/gather | solution.py:62
  7.5 0.0 copy-start.8
  7.5 0.0 copy-start.1
  7.5 0.0 copy-start.6
  7.5 1.2 %select_select_fusion = bf16[64,16,512]{2,1,0:T(8,128)(2,1)} fusion(bf16[64,16,512]{2,1,0:T(8,128)(2,1)S(1)} %bitcast.33, pred[64,16]{1,0:T(8,128)(4,1)S(1)} %copy.31, pred[64,16]{1,0:T(8,128)(4,1)S(1)} %iota_compare_fusion.4), kind=kLoop, calls=%fused_computation.26 | loop fusion | flops 1048576 | bytes 2099200 | tf_op jit(solution)/shard_map/jit(_where)/select_n | solution.py:64
  8.8 24.2 %all-to-all-start = ((bf16[64,16,512]{2,1,0:T(8,128)(2,1)}), bf16[64,16,512]{2,1,0:T(8,128)(2,1)}, u32[]{:S(2)}, u32[]{:S(2)}) async-start(bf16[64,16,512]{2,1,0:T(8,128)(2,1)} %select_select_fusion), calls=%async_computation | async-start | bytes 2097152 | tf_op jit(solution)/shard_map/all_to_all | solution.py:68
  33.0 0.2 fusion.22
  33.2 0.0 copy-start.3
  33.3 2.3 %gather_fusion.2 = f32[512,512]{1,0:T(8,128)} fusion(f32[32,512]{1,0:T(8,128)S(1)} %fusion.22, s32[1024]{0:T(1024)S(1)} %pad_clamp_fusion.2), kind=kCustom, calls=%fused_computation.clone | custom fusion | bytes 2099200 | tf_op jit(solution)/shard_map/jit(_take)/gather | solution.py:21
  35.7 0.2 fusion.25
  35.8 24.4 %all-to-all-done = bf16[64,16,512]{2,1,0:T(8,128)(2,1)} async-done(((bf16[64,16,512]{2,1,0:T(8,128)(2,1)}), bf16[64,16,512]{2,1,0:T(8,128)(2,1)}, u32[]{:S(2)}, u32[]{:S(2)}) %all-to-all-start) | async-done | bytes 1048608 | tf_op jit(solution)/shard_map/all_to_all | solution.py:68
  60.3 2.1 %fusion.10 = f32[64,16,512]{2,1,0:T(8,128)S(1)} fusion(bf16[64,16,512]{2,1,0:T(8,128)(2,1)} %all-to-all-done, bf16[1024,512]{1,0:T(8,128)(2,1)} %param.38), kind=kOutput, calls=%fused_computation.27 | convolution fusion | flops 536870912 | bytes 3670016 | tf_op jit(solution)/shard_map/psd,dh->psh/dot_general | solution.py:66
  62.3 0.0 copy-start.17
  62.3 0.0 copy-start.18
  62.3 0.0 copy-start.19
  62.4 2.3 %gather_fusion.1 = f32[512,512]{1,0:T(8,128)} fusion(f32[1024,512]{1,0:T(8,128)S(1)} %bitcast.32, s32[1024]{0:T(1024)S(1)} %pad_clamp_fusion.3), kind=kCustom, calls=%fused_computation.4 | custom fusion | bytes 2099200 | tf_op jit(solution)/shard_map/jit(_take)/gather | solution.py:21
  64.7 0.0 copy-start.4
  64.7 0.0 copy-start.11
  64.7 0.0 copy-start.12
  64.7 0.0 copy-start.13
  64.7 2.4 %fusion.6 = bf16[32,512]{1,0:T(8,128)(2,1)S(1)} fusion(bf16[512,512]{1,0:T(8,128)(2,1)S(1)} %copy-done.17, f32[512]{0:T(512)S(1)} %copy-done.18, f32[512,512]{1,0:T(8,128)} %gather_fusion.2, f32[512,512]{1,0:T(8,128)} %gather_fusion.1, f32[512]{0:T(512)S(1)} %copy-done.19, pred[512]{0:T(512)(128)(4,1)S(1)} %get-tuple-element.10, ...), kind=kOutput, calls=%fused_computation.18 | convolution fusion | flops 288129024 | bytes 2661376 | tf_op jit(solution)/shard_map/em,ed->md/dot_general | solution.py:27
  67.2 0.0 copy-start.10
  67.2 0.0 copy-start.2
  67.2 0.5 fusion.55
  67.7 0.2 multiply_reduce_fusion.1
  67.9 0.1 add_convert_fusion.1
  68.0 0.8 broadcast_in_dim.47
  68.9 4.7 %scatter_fusion = bf16[16,32,512]{2,1,0:T(8,128)(2,1)} fusion(bf16[16,32,512]{2,1,0:T(8,128)(2,1)} %broadcast_in_dim.47, s32[32]{0:T(128)S(1)} %fusion.44, bf16[32,512]{1,0:T(8,128)(2,1)S(1)} %add_convert_fusion.1), kind=kCustom, calls=%fused_computation.5 | custom fusion | bytes 98560 | tf_op jit(solution)/shard_map/scatter | solution.py:91
  73.6 10.1 %all-to-all-start.1 = ((bf16[16,32,512]{2,1,0:T(8,128)(2,1)}), bf16[16,32,512]{2,1,0:T(8,128)(2,1)S(1)}, u32[]{:S(2)}, u32[]{:S(2)}) async-start(bf16[16,32,512]{2,1,0:T(8,128)(2,1)} %scatter_fusion), calls=%async_computation.1 | async-start | bytes 1048576 | tf_op jit(solution)/shard_map/all_to_all | solution.py:93
  83.8 17.2 %all-to-all-done.1 = bf16[16,32,512]{2,1,0:T(8,128)(2,1)S(1)} async-done(((bf16[16,32,512]{2,1,0:T(8,128)(2,1)}), bf16[16,32,512]{2,1,0:T(8,128)(2,1)S(1)}, u32[]{:S(2)}, u32[]{:S(2)}) %all-to-all-start.1) | async-done | bytes 524320 | tf_op jit(solution)/shard_map/all_to_all | solution.py:93
  101.0 0.1 reduce_sum.50
  101.1 0.2 fusion.16
  101.3 1.2 %fusion.14 = f32[32,512]{1,0:T(8,128)S(1)} fusion(bf16[32,512]{1,0:T(8,128)(2,1)S(1)} %reduce_sum.50, bf16[1024,512]{1,0:T(8,128)(2,1)} %param.47), kind=kOutput, calls=%fused_computation.31 | convolution fusion | flops 16777216 | bytes 622592 | tf_op jit(solution)/shard_map/dot_general | solution.py:96
  102.5 1.2 %fusion.18 = f32[32,512]{1,0:T(8,128)S(1)} fusion(bf16[32,512]{1,0:T(8,128)(2,1)S(1)} %reduce_sum.50, bf16[1024,512]{1,0:T(8,128)(2,1)} %param.51), kind=kOutput, calls=%fused_computation.35 | convolution fusion | flops 16777216 | bytes 622592 | tf_op jit(solution)/shard_map/dot_general | solution.py:10
  103.8 1.6 %gather_fusion.3 = f32[512,512]{1,0:T(8,128)S(1)} fusion(f32[32,512]{1,0:T(8,128)S(1)} %fusion.16, s32[1024]{0:T(1024)S(1)} %pad_clamp_fusion.1), kind=kCustom, calls=%fused_computation.1.clone | custom fusion | bytes 2099200 | tf_op jit(solution)/shard_map/jit(_take)/gather | solution.py:21
  105.4 0.0 copy-start.20
  105.4 1.6 %gather_fusion.4 = f32[512,512]{1,0:T(8,128)S(1)} fusion(f32[32,512]{1,0:T(8,128)S(1)} %fusion.14, s32[1024]{0:T(1024)S(1)} %pad_clamp_fusion), kind=kCustom, calls=%fused_computation.2.clone | custom fusion | bytes 2099200 | tf_op jit(solution)/shard_map/jit(_take)/gather | solution.py:21
  107.1 0.0 copy-start.5
  107.1 0.0 copy-start.16
  107.1 1.8 %fusion.7 = bf16[32,512]{1,0:T(8,128)(2,1)S(1)} fusion(bf16[512,512]{1,0:T(8,128)(2,1)} %param.49, f32[512]{0:T(512)S(1)} %copy-done.20, f32[512,512]{1,0:T(8,128)S(1)} %gather_fusion.4, f32[512,512]{1,0:T(8,128)S(1)} %gather_fusion.3, f32[512]{0:T(512)S(1)} %copy-done.21, pred[512]{0:T(512)(128)(4,1)S(1)} %get-tuple-element.12, ...), kind=kOutput, calls=%fused_computation.19 | convolution fusion | flops 288129024 | bytes 2661376 | tf_op jit(solution)/shard_map/em,ed->md/dot_general | solution.py:27
  109.0 1.5 %fusion.58 = (f32[32]{0:T(128)S(1)}, f32[32,512]{1,0:T(8,128)S(1)}) fusion(f32[512]{0:T(512)S(1)} %copy-done.14, bf16[512,512]{1,0:T(8,128)(2,1)S(1)} %copy-done.5, f32[32,512]{1,0:T(8,128)S(1)} %fusion.18, bf16[32,512]{1,0:T(8,128)(2,1)S(1)} %fusion.7, bf16[1024,512]{1,0:T(8,128)(2,1)} %param.51, f32[512]{0:T(512)S(1)} %copy-done.15), kind=kOutput, calls=%fused_computation.100 | convolution fusion | flops 33701856 | bytes 1216640 | tf_op jit(solution)/shard_map/dot_general | solution.py:13
  110.6 0.2 multiply_reduce_fusion
  110.8 0.7 add_convert_fusion
  (47 shorter events, 0.2 us)
Async XLA Ops:
  0.0 67.1 %copy-start = (bf16[512,512]{1,0:T(8,128)(2,1)S(1)}, bf16[512,512]{1,0:T(8,128)(2,1)}, u32[]{:S(2)}) copy-start(bf16[512,512]{1,0:T(8,128)(2,1)} %param.44) | copy-start | bytes 1572868
  7.5 25.5 %copy-start.8 = (s32[512]{0:T(512)S(1)}, s32[512]{0:T(512)}, u32[]{:S(2)}) copy-start(s32[512]{0:T(512)} %param.34) | copy-start | bytes 6148
  7.5 25.5 %copy-start.1 = (bf16[1024,512]{1,0:T(8,128)(2,1)S(1)}, bf16[1024,512]{1,0:T(8,128)(2,1)}, u32[]{:S(2)}) copy-start(bf16[1024,512]{1,0:T(8,128)(2,1)} %param.38) | copy-start | bytes 3145732
  7.5 25.5 %copy-start.6 = (bf16[32,512]{1,0:T(8,128)(2,1)S(1)}, bf16[32,512]{1,0:T(8,128)(2,1)}, u32[]{:S(2)}) copy-start(bf16[32,512]{1,0:T(8,128)(2,1)} %param.30) | copy-start | bytes 98308
  8.8 51.5 %all-to-all-start = ((bf16[64,16,512]{2,1,0:T(8,128)(2,1)}), bf16[64,16,512]{2,1,0:T(8,128)(2,1)}, u32[]{:S(2)}, u32[]{:S(2)}) async-start(bf16[64,16,512]{2,1,0:T(8,128)(2,1)} %select_select_fusion), calls=%async_computation | async-start | bytes 2097152 | tf_op jit(solution)/shard_map/all_to_all | solution.py:68
  33.2 2.4 %copy-start.7 = (s32[512]{0:T(512)S(1)}, s32[512]{0:T(512)}, u32[]{:S(2)}) copy-start(s32[512]{0:T(512)} %param.33) | copy-start | bytes 6148
  33.2 2.4 %copy-start.22 = (s32[32]{0:T(128)S(1)}, s32[32]{0:T(128)}, u32[]{:S(2)}) copy-start(s32[32]{0:T(128)} %param.35) | copy-start | bytes 388
  33.2 2.4 %copy-start.3 = (bf16[1024,512]{1,0:T(8,128)(2,1)S(1)}, bf16[1024,512]{1,0:T(8,128)(2,1)}, u32[]{:S(2)}) copy-start(bf16[1024,512]{1,0:T(8,128)(2,1)} %param.42) | copy-start | bytes 3145732
  62.3 2.4 %copy-start.17 = (bf16[512,512]{1,0:T(8,128)(2,1)S(1)}, bf16[512,512]{1,0:T(8,128)(2,1)}, u32[]{:S(2)}) copy-start(bf16[512,512]{1,0:T(8,128)(2,1)} %param.40) | copy-start | bytes 1572868
  62.3 2.4 %copy-start.18 = (f32[512]{0:T(512)S(1)}, f32[512]{0:T(512)}, u32[]{:S(2)}) copy-start(f32[512]{0:T(512)} %param.41) | copy-start | bytes 6148
  62.3 2.4 %copy-start.19 = (f32[512]{0:T(512)S(1)}, f32[512]{0:T(512)}, u32[]{:S(2)}) copy-start(f32[512]{0:T(512)} %param.39) | copy-start | bytes 6148
  64.7 2.5 %copy-start.4 = (bf16[1024,512]{1,0:T(8,128)(2,1)S(1)}, bf16[1024,512]{1,0:T(8,128)(2,1)}, u32[]{:S(2)}) copy-start(bf16[1024,512]{1,0:T(8,128)(2,1)} %param.42) | copy-start | bytes 3145732
  64.7 2.4 %copy-start.11 = (f32[512]{0:T(512)S(1)}, f32[512]{0:T(512)}, u32[]{:S(2)}) copy-start(f32[512]{0:T(512)} %param.45) | copy-start | bytes 6148
  64.7 2.4 %copy-start.12 = (f32[512]{0:T(512)S(1)}, f32[512]{0:T(512)}, u32[]{:S(2)}) copy-start(f32[512]{0:T(512)} %param.43) | copy-start | bytes 6148
  64.7 3.2 %copy-start.13 = (f32[512]{0:T(512)S(1)}, f32[512]{0:T(512)}, u32[]{:S(2)}) copy-start(f32[512]{0:T(512)} %param.46) | copy-start | bytes 6148
  67.2 16.5 %copy-start.9 = (s32[512]{0:T(512)S(1)}, s32[512]{0:T(512)}, u32[]{:S(2)}) copy-start(s32[512]{0:T(512)} %param.36) | copy-start | bytes 6148
  67.2 16.5 %copy-start.10 = (s32[512]{0:T(512)S(1)}, s32[512]{0:T(512)}, u32[]{:S(2)}) copy-start(s32[512]{0:T(512)} %param.37) | copy-start | bytes 6148
  67.2 33.9 %copy-start.2 = (bf16[1024,512]{1,0:T(8,128)(2,1)S(1)}, bf16[1024,512]{1,0:T(8,128)(2,1)}, u32[]{:S(2)}) copy-start(bf16[1024,512]{1,0:T(8,128)(2,1)} %param.47) | copy-start | bytes 3145732
  73.6 27.5 %all-to-all-start.1 = ((bf16[16,32,512]{2,1,0:T(8,128)(2,1)}), bf16[16,32,512]{2,1,0:T(8,128)(2,1)S(1)}, u32[]{:S(2)}, u32[]{:S(2)}) async-start(bf16[16,32,512]{2,1,0:T(8,128)(2,1)} %scatter_fusion), calls=%async_computation.1 | async-start | bytes 1048576 | tf_op jit(solution)/shard_map/all_to_all | solution.py:93
  105.4 1.7 %copy-start.20 = (f32[512]{0:T(512)S(1)}, f32[512]{0:T(512)}, u32[]{:S(2)}) copy-start(f32[512]{0:T(512)} %param.50) | copy-start | bytes 6148
  105.4 1.7 %copy-start.21 = (f32[512]{0:T(512)S(1)}, f32[512]{0:T(512)}, u32[]{:S(2)}) copy-start(f32[512]{0:T(512)} %param.48) | copy-start | bytes 6148
  107.1 1.9 %copy-start.5 = (bf16[512,512]{1,0:T(8,128)(2,1)S(1)}, bf16[512,512]{1,0:T(8,128)(2,1)}, u32[]{:S(2)}) copy-start(bf16[512,512]{1,0:T(8,128)(2,1)} %param.53) | copy-start | bytes 1572868
  107.1 1.9 %copy-start.14 = (f32[512]{0:T(512)S(1)}, f32[512]{0:T(512)}, u32[]{:S(2)}) copy-start(f32[512]{0:T(512)} %param.54) | copy-start | bytes 6148
  107.1 1.9 %copy-start.15 = (f32[512]{0:T(512)S(1)}, f32[512]{0:T(512)}, u32[]{:S(2)}) copy-start(f32[512]{0:T(512)} %param.52) | copy-start | bytes 6148
  107.1 3.6 %copy-start.16 = (f32[512]{0:T(512)S(1)}, f32[512]{0:T(512)}, u32[]{:S(2)}) copy-start(f32[512]{0:T(512)} %param.55) | copy-start | bytes 6148
where the time goes:
time: 112 us; the launch traced here: 111 us
  waiting for transfers between devices  41.6 us (37%)
  starting transfers between devices  34.4 us (31%)
  local copies, waits for them, and re-layouts  19.6 us (18%)
  matrix products  11.3 us (10%)
  other arithmetic  4.02 us (4%)
    all_to_all x1, waiting for transfers between devices, shards(): lax.all_to_all(picked, 'dom', split_axis=0, concat_axis=0, tiled=True)  24.4 us
    all_to_all x1, starting transfers between devices, shards(): lax.all_to_all(picked, 'dom', split_axis=0, concat_axis=0, tiled=True)  24.2 us
    all_to_all x1, waiting for transfers between devices, shards(): lax.all_to_all(buckets, 'band', split_axis=0, concat_axis=0, tiled=True)  17.2 us
    all_to_all x1, starting transfers between devices, shards(): lax.all_to_all(buckets, 'band', split_axis=0, concat_axis=0, tiled=True)  10.1 us
    gather x1, local copies, waits for them, and re-layouts, shards(): jnp.take(grid_latent, send_rows.reshape(-1), axis=0)  4.98 us
    scatter x1, local copies, waits for them, and re-layouts, shards(): jnp.zeros((bands, rows_here, width), jnp.bfloat16).at[dest_band, dest_slot]  4.71 us
    dot_general x2, matrix products, edge_sum(): jnp.einsum('em,ed->md', one_hot, message, preferred_element_type=jnp.floa...  4.23 us
    gather x2, local copies, waits for them, and re-layouts, edge_sum(): jnp.take(send_proj, sender, axis=0) + jnp.take(recv_proj, receiver, axis=0)  3.96 us
  transfers between devices with their start and end apart: 2, of which 2 were waited for; matrix products, arithmetic and copies ran while one was open for 2% of the time, Pallas kernels for 0%

commit v1 on v0

v1 whole, which is shorter than its diff:
```python
import functools

import jax
import jax.numpy as jnp
import numpy as np
from jax import lax
from jax.experimental import pallas as pl
from jax.experimental.pallas import tpu as pltpu
from jax.sharding import PartitionSpec as P

MESH = pl.DeviceIdType.MESH
F32 = jnp.float32
BF16 = jnp.bfloat16
I32 = jnp.int32
CAP = 16
MOVE = 8
WEIGHTS = 8


def iota(shape, dim):
    return lax.broadcasted_iota(I32, shape, dim)


def dot(a, b):
    return jnp.dot(a, b, preferred_element_type=F32)


def one_hot(mask):
    return jnp.where(mask, 1.0, 0.0).astype(BF16)


def silu(v):
    return v / (1.0 + jnp.exp(-v))


def halves(v):
    high = v.astype(BF16)
    return jnp.concatenate([high, (v - high.astype(F32)).astype(BF16)], axis=0)


def node_out(rows, pre, agg, w1, w2, b2, gain):
    width = rows.shape[1]
    z = silu(pre + dot(agg, w1[width:])).astype(BF16)
    u = dot(z, w2[...]) + b2
    center = u - jnp.mean(u, axis=-1, keepdims=True)
    spread = jnp.mean(center * center, axis=-1, keepdims=True)
    return (rows.astype(F32) + gain * (center * lax.rsqrt(spread + 1e-05))).astype(BF16)


def aggregate(hidden, hot_t, w2, b2):
    rows = hot_t.shape[0]
    two = dot(halves(dot(hot_t, hidden)), w2[...])
    count = jnp.sum(hot_t.astype(F32), axis=1, keepdims=True)
    return (two[:rows] + two[rows:] + count * b2).astype(BF16)


def lanes_to_rows(row):
    return jnp.broadcast_to(row, (128, row.shape[1])).T


def kernel(
    bands, zs, ys, order,
    grid, rows, send_rows, send_count, enc_s, enc_r, move_to, proc_s, proc_r,
    e_b1, e_b2, en_b1, en_b2, e_gain, p_b1, p_b2, pn_b1, pn_b2, p_gain,
    *rest,
):
    hbm, out = rest[:WEIGHTS], rest[WEIGHTS]
    held = rest[WEIGHTS + 1 : 2 * WEIGHTS + 1]
    (send, recv, pick, base, total, meta_out, meta_in, move_out, move_in,
     w_sem, ss, rs, ms, mr, vs, vr) = rest[2 * WEIGHTS + 1 :]
    e_w1, e_w2, n_w1, n_w2, p_w1, p_w2, q_w1, q_w2 = held
    doms = zs * ys
    width = grid.shape[1]
    count = rows.shape[0]
    edges = enc_s.shape[1]
    slots = doms * CAP
    chunks = rs.shape[0]
    per = doms // chunks
    band, dom = lax.axis_index("band"), lax.axis_index("dom")
    z, y = dom // ys, dom % ys

    barrier = pltpu.get_barrier_semaphore()
    for a, c in order:
        there = ((z + a) % zs) * ys + (y + c) % ys
        pl.semaphore_signal(barrier, inc=1, device_id=(band, there), device_id_type=MESH)
    for k in range(1, bands):
        pl.semaphore_signal(barrier, inc=1, device_id=((band + k) % bands, dom), device_id_type=MESH)

    loads = [pltpu.make_async_copy(hbm[i], held[i], w_sem.at[i]) for i in range(WEIGHTS)]
    for load in loads:
        load.start()

    block = min(256, slots)
    listed = send_rows[...].astype(F32).astype(BF16)
    counts = send_count[...].astype(F32)

    def gather(i, carry):
        slot = iota((block, doms), 0) + i * block
        rel = slot // CAP
        there = ((z + rel // ys) % zs) * ys + (y + rel % ys) % ys
        peer = there == iota((block, doms), 1)
        mine = dot(one_hot(peer), listed)
        lane = (iota((block, CAP), 0) % CAP) == iota((block, CAP), 1)
        index = dot(jnp.where(lane, mine, 0.0).astype(BF16), jnp.ones((CAP, grid.shape[0]), BF16))
        limit = dot(jnp.where(peer, counts, 0.0).astype(BF16), jnp.ones((doms, grid.shape[0]), BF16))
        at = iota((block, grid.shape[0]), 0) % CAP
        hot = (index == iota((block, grid.shape[0]), 1).astype(F32)) & (at.astype(F32) < limit)
        send[pl.ds(pl.multiple_of(i * block, block), block), :] = dot(one_hot(hot), grid[...]).astype(BF16)
        return carry

    lax.fori_loop(0, slots // block, gather, 0)

    dest = move_to[...]
    leaves = (dest // count) != band
    before = one_hot(iota((count, count), 0) < iota((count, count), 1))
    rank = dot(jnp.broadcast_to(one_hot(leaves), (8, count)), before)[:MOVE]
    packs = (rank == iota((MOVE, count), 0).astype(F32)) & leaves
    goes = jnp.sum(jnp.where(packs, (dest + 1).astype(F32), 0.0), axis=1, keepdims=True) - 1.0
    goes = jnp.broadcast_to(goes, (MOVE, 128)).astype(I32)
    meta_out[...] = jnp.concatenate([goes, goes], axis=0)
    meta_in[0] = jnp.full((2 * MOVE, 128), -1, I32)
    move_in[0] = jnp.zeros((2 * MOVE, width // 2), BF16)

    pl.semaphore_wait(barrier, len(order) + bands - 1)

    for a, c in order:
        there = ((z + a) % zs) * ys + (y + c) % ys
        at = (a * ys + c) * CAP
        pltpu.make_async_remote_copy(
            send.at[pl.ds(at, CAP)], recv.at[pl.ds(at, CAP)], ss.at[0], rs.at[(a * ys + c) // per],
            device_id=(band, there), device_id_type=MESH,
        ).start()
    for k in range(1, bands):
        pltpu.make_async_remote_copy(
            meta_out, meta_in.at[k], ms.at[0], mr.at[0],
            device_id=((band + k) % bands, dom), device_id_type=MESH,
        ).start()
    recv[pl.ds(0, CAP), :] = send[pl.ds(0, CAP), :]

    sender = enc_s[...]
    from_dom = sender // CAP
    rel_z = (z - from_dom // ys + zs) % zs
    rel_y = (y - from_dom % ys + ys) % ys
    place = lanes_to_rows((rel_z * ys + rel_y) * CAP + sender % CAP)
    for i in range(slots // 128):
        pick[:, pl.ds(i * 128, 128)] = one_hot(place == iota((edges, 128), 1) + i * 128)
    lane = iota((edges, 128), 1)
    receiver = lanes_to_rows(enc_r[...])
    recv_hot = one_hot(((lane % count) == receiver) & (lane < 2 * count))
    hot_t = one_hot(iota((count, edges), 0) == enc_r[...])
    loads[0].wait()
    recv_proj = dot(rows[...], e_w1[width:]) + e_b1[...]
    stack = jnp.concatenate([halves(recv_proj), jnp.zeros((128 - 2 * count, recv_proj.shape[1]), BF16)], axis=0)
    base[...] = dot(recv_hot, stack)
    loads[2].wait()
    node_pre = dot(rows[...], n_w1[:width]) + en_b1[...]
    proc_send, proc_recv = lanes_to_rows(proc_s[...]), lanes_to_rows(proc_r[...])
    proc_hot = one_hot((lane % count) == jnp.where((lane // count) % 2 == 0, proc_send, proc_recv))
    proc_hot_t = one_hot(iota((count, edges), 0) == proc_r[...])
    pack = one_hot(packs)
    stays = one_hot(dest - band * count == iota((count, count), 0))
    pltpu.make_async_remote_copy(
        meta_in.at[pl.ds(1, bands - 1)], meta_in.at[pl.ds(1, bands - 1)], ms.at[0], mr.at[0],
        device_id=((band + 1) % bands, dom), device_id_type=MESH,
    ).wait()
    moved = meta_in[...].reshape(bands * 2 * MOVE, 128)
    moved = jnp.concatenate([moved[i * 128 : (i + 1) * 128].T for i in range(bands * 2 * MOVE // 128)], axis=1)
    lands = moved[:count] == iota((count, bands * 2 * MOVE), 0) + band * count
    left = (iota((count, bands * 2 * MOVE), 1) % (2 * MOVE)) < MOVE
    place_in = jnp.concatenate([one_hot(lands & left), one_hot(lands & jnp.logical_not(left))], axis=0)
    for i in (1, 3, 4, 5, 6, 7):
        loads[i].wait()

    span = per * CAP
    for i in range(chunks):
        first = 1 if i == 0 else i * per
        blocks = per - 1 if i == 0 else per
        landed = recv.at[pl.ds(first * CAP, blocks * CAP)]
        pltpu.make_async_remote_copy(
            landed, landed, ss.at[0], rs.at[i], device_id=(band, (z * ys + (y + 1) % ys)), device_id_type=MESH
        ).wait_recv()
        part = dot(pick[:, pl.ds(i * span, span)], recv[pl.ds(i * span, span), :])
        if i == 0:
            total[...] = part
        elif i < chunks - 1:
            total[...] += part
    gathered = (total[...] + part).astype(BF16) if chunks > 1 else part.astype(BF16)
    hidden = silu(base[...] + dot(gathered, e_w1[:width])).astype(BF16)
    agg = aggregate(hidden, hot_t, e_w2, e_b2[...])
    mesh_enc = node_out(rows[...], node_pre, agg, n_w1, n_w2, en_b2[...], e_gain[...])

    packed = dot(pack, mesh_enc)
    move_out[...] = jnp.concatenate([packed[:, : width // 2], packed[:, width // 2 :]], axis=0).astype(BF16)
    for k in range(1, bands):
        pltpu.make_async_remote_copy(
            move_out, move_in.at[k], vs.at[0], vr.at[0],
            device_id=((band + k) % bands, dom), device_id_type=MESH,
        ).start()
    kept = dot(stays, mesh_enc)
    pltpu.make_async_remote_copy(
        move_in.at[pl.ds(1, bands - 1)], move_in.at[pl.ds(1, bands - 1)], vs.at[0], vr.at[0],
        device_id=((band + 1) % bands, dom), device_id_type=MESH,
    ).wait()
    came = dot(place_in, move_in[...].reshape(bands * 2 * MOVE, width // 2))
    proc_in = (kept + jnp.concatenate([came[:count], came[count:]], axis=1)).astype(BF16)

    projected = jnp.concatenate([dot(proc_in, p_w1[:width]), dot(proc_in, p_w1[width:]) + p_b1[...]], axis=0)
    hidden = silu(dot(proc_hot, halves(projected))).astype(BF16)
    node_pre = dot(proc_in, q_w1[:width]) + pn_b1[...]
    agg = aggregate(hidden, proc_hot_t, p_w2, p_b2[...])
    out[...] = node_out(proc_in, node_pre, agg, q_w1, q_w2, pn_b2[...], p_gain[...])
    outgoing = send.at[pl.ds(CAP, slots - CAP)]
    pltpu.make_async_remote_copy(
        outgoing, outgoing, ss.at[0], rs.at[0], device_id=(band, (z * ys + (y + 1) % ys)), device_id_type=MESH
    ).wait_send()


def solution(mesh):
    bands, doms = mesh.shape["band"], mesh.shape["dom"]
    zs = 2 ** ((doms.bit_length() - 1) // 2)
    ys = doms // zs
    offsets = [(a, c) for a in range(zs) for c in range(ys) if (a, c) != (0, 0)]
    order = [offsets[i] for i in np.random.RandomState(0).permutation(len(offsets))]

    def shards(
        grid_latent, mesh_latent, send_rows, send_count, enc_sender, enc_receiver, move_to, proc_sender, proc_receiver,
        enc_edge_w1, enc_edge_b1, enc_edge_w2, enc_edge_b2, enc_node_w1, enc_node_b1, enc_node_w2, enc_node_b2, enc_gain,
        proc_edge_w1, proc_edge_b1, proc_edge_w2, proc_edge_b2, proc_node_w1, proc_node_b1, proc_node_w2, proc_node_b2, proc_gain,
    ):
        count, width = mesh_latent.shape
        edges = enc_sender.shape[0]
        slots = doms * CAP
        weights = (enc_edge_w1, enc_edge_w2, enc_node_w1, enc_node_w2, proc_edge_w1, proc_edge_w2, proc_node_w1, proc_node_w2)
        small = (send_count, enc_sender, enc_receiver, move_to, proc_sender, proc_receiver,
                 enc_edge_b1, enc_edge_b2, enc_node_b1, enc_node_b2, enc_gain,
                 proc_edge_b1, proc_edge_b2, proc_node_b1, proc_node_b2, proc_gain)
        small = [a.reshape(1, -1) for a in small]
        vmem = pl.BlockSpec(memory_space=pltpu.VMEM)
        dma = pltpu.SemaphoreType.DMA
        chunks = max(1, slots // 256)
        return pl.pallas_call(
            functools.partial(kernel, bands, zs, ys, order),
            out_shape=jax.ShapeDtypeStruct((count, width), BF16),
            in_specs=[vmem] * (3 + len(small)) + [pl.BlockSpec(memory_space=pl.ANY)] * WEIGHTS,
            out_specs=vmem,
            scratch_shapes=[pltpu.VMEM(w.shape, w.dtype) for w in weights] + [
                pltpu.VMEM((slots, width), BF16),
                pltpu.VMEM((slots, width), BF16),
                pltpu.VMEM((edges, slots), BF16),
                pltpu.VMEM((edges, enc_edge_w1.shape[1]), F32),
                pltpu.VMEM((edges, width), F32),
                pltpu.VMEM((2 * MOVE, 128), I32),
                pltpu.VMEM((bands, 2 * MOVE, 128), I32),
                pltpu.VMEM((2 * MOVE, width // 2), BF16),
                pltpu.VMEM((bands, 2 * MOVE, width // 2), BF16),
                dma((WEIGHTS,)), dma((1,)), dma((chunks,)), dma((1,)), dma((1,)), dma((1,)), dma((1,)),
            ],
            compiler_params=pltpu.CompilerParams(
                collective_id=0, has_side_effects=True, vmem_limit_bytes=40 * 1024 * 1024
            ),
            name="encode_process",
        )(grid_latent, mesh_latent, send_rows, *small, *weights)

    split, whole = P(("band", "dom")), P()
    return jax.shard_map(
        shards,
        mesh=mesh,
        in_specs=(P(("band", "dom"), None),) * 3 + (split,) * 6 + (whole,) * 18,
        out_specs=P(("band", "dom"), None),
        check_vma=False,
    )
```

time: 112 us -> 74.6 us (0.67)
  Pallas kernels: 0 us -> 61.8 us
  waiting for transfers between devices: 41.6 us -> 0 us
  starting transfers between devices: 34.4 us -> 0 us
  matrix products: 11.3 us -> 0 us
  local copies, waits for them, and re-layouts: 19.6 us -> 12.1 us
  other arithmetic: 4.02 us -> 0 us
    pallas_call x0 -> x1, Pallas kernels: none -> 61.8 us  [shards(): pl.pallas_call(functools.partial(kernel, bands, zs, ys, order), out_shape...]
    all_to_all x2 -> x0, waiting for transfers between devices: 41.6 us -> none  [the longest x1 24.4 us: shards(): lax.all_to_all(picked, 'dom', split_axis=0, concat_axis=0, tiled=True)]
    all_to_all x2 -> x0, starting transfers between devices: 34.4 us -> none  [the longest x1 24.2 us: shards(): lax.all_to_all(picked, 'dom', split_axis=0, concat_axis=0, tiled=True)]
    gather x5 -> x0, local copies, waits for them, and re-layouts: 12.9 us -> none  [the longest x1 4.98 us: shards(): jnp.take(grid_latent, send_rows.reshape(-1), axis=0)]
    dot_general x10 -> x0, matrix products: 11.3 us -> none  [the longest x2 4.23 us: edge_sum(): jnp.einsum('em,ed->md', one_hot, message, preferred_element_type=jnp.floa...]
    unnamed x47 -> x56, local copies, waits for them, and re-layouts: 0.97 us -> 12.1 us
    scatter x1 -> x0, local copies, waits for them, and re-layouts: 4.71 us -> none  [shards(): jnp.zeros((bands, rows_here, width), jnp.bfloat16).at[dest_band, dest_slot]]
    select_n x6 -> x0, other arithmetic: 1.27 us -> none  [the longest x1 1.24 us: shards(): picked = jnp.where(keep[:, :, None], picked, jnp.zeros_like(picked))]
  transfers between devices with their start and end apart: 2 -> 0, of which waited for: 2 -> 0; matrix products, arithmetic and copies ran while one was open for 2% -> 0% of each run, Pallas kernels for 0% -> 0%
where the time goes in v1:
time: 74.6 us; the launch traced here: 74 us
  Pallas kernels  61.8 us (83%)
  local copies, waits for them, and re-layouts  12.1 us (16%)
    pallas_call x1, Pallas kernels, shards(): pl.pallas_call(functools.partial(kernel, bands, zs, ys, order), out_shape...  61.8 us
    unnamed x56, local copies, waits for them, and re-layouts  12.1 us

profile of v1, /device:TPU:1, one launch (start us, length us, event | category | flops | bytes accessed | tf_op | source)
XLA Modules:
  0.0 74.0 jit_solution(3844451243488272706)
XLA Ops:
  0.0 0.0 copy-start.26
  0.0 0.0 copy-start.9
  0.0 0.7 copy-done.26
  0.7 0.0 copy-start.10
  0.7 0.0 copy-start.11
  0.7 0.0 copy-start.12
  0.7 0.0 copy-start.13
  0.7 0.0 copy-start.14
  0.7 0.0 copy-start.15
  0.7 0.0 copy-start.16
  0.7 0.0 copy-start.17
  0.7 0.0 copy-start.18
  0.8 0.0 copy-start.19
  0.8 0.0 copy-start.20
  0.8 0.0 copy-start.21
  0.8 0.0 copy-start.22
  0.8 0.0 copy-start.23
  0.8 0.0 copy-start.24
  0.8 0.0 copy-start.25
  0.8 0.1 copy.28.send_rows
  0.9 0.0 copy-done.9
  0.9 0.5 copy-done.10
  1.4 0.0 copy-done.11
  1.4 0.0 copy-done.12
  1.4 0.0 copy-done.13
  1.4 0.0 copy-done.14
  1.4 0.0 copy-done.15
  1.5 0.0 copy-done.16
  1.5 0.0 copy-done.17
  1.5 0.0 copy-done.18
  1.5 0.0 copy-done.19
  1.5 0.0 copy-done.20
  1.5 0.0 copy-done.21
  1.6 0.0 copy-done.22
  1.6 0.0 copy-done.23
  1.6 0.0 copy-done.24
  1.6 0.0 copy-done.25
  1.6 1.2 %copy-done = bf16[1024,512]{1,0:T(8,128)(2,1)S(1)} copy-done((bf16[1024,512]{1,0:T(8,128)(2,1)S(1)}, bf16[1024,512]{1,0:T(8,128)(2,1)}, u32[]{:S(2)}) %copy-start) | copy-done | bytes 1048600
  2.8 1.2 %copy-done.1 = bf16[1024,512]{1,0:T(8,128)(2,1)S(1)} copy-done((bf16[1024,512]{1,0:T(8,128)(2,1)S(1)}, bf16[1024,512]{1,0:T(8,128)(2,1)}, u32[]{:S(2)}) %copy-start.1) | copy-done | bytes 1048600
  4.0 1.2 %copy-done.2 = bf16[1024,512]{1,0:T(8,128)(2,1)S(1)} copy-done((bf16[1024,512]{1,0:T(8,128)(2,1)S(1)}, bf16[1024,512]{1,0:T(8,128)(2,1)}, u32[]{:S(2)}) %copy-start.2) | copy-done | bytes 1048600
  5.3 1.2 %copy-done.3 = bf16[1024,512]{1,0:T(8,128)(2,1)S(1)} copy-done((bf16[1024,512]{1,0:T(8,128)(2,1)S(1)}, bf16[1024,512]{1,0:T(8,128)(2,1)}, u32[]{:S(2)}) %copy-start.3) | copy-done | bytes 1048600
  6.5 1.0 %copy-done.4 = bf16[512,512]{1,0:T(8,128)(2,1)S(1)} copy-done((bf16[512,512]{1,0:T(8,128)(2,1)S(1)}, bf16[512,512]{1,0:T(8,128)(2,1)}, u32[]{:S(2)}) %copy-start.4) | copy-done | bytes 524312
  7.5 1.0 %copy-done.5 = bf16[512,512]{1,0:T(8,128)(2,1)S(1)} copy-done((bf16[512,512]{1,0:T(8,128)(2,1)S(1)}, bf16[512,512]{1,0:T(8,128)(2,1)}, u32[]{:S(2)}) %copy-start.5) | copy-done | bytes 524312
  8.6 1.0 %copy-done.6 = bf16[512,512]{1,0:T(8,128)(2,1)S(1)} copy-done((bf16[512,512]{1,0:T(8,128)(2,1)S(1)}, bf16[512,512]{1,0:T(8,128)(2,1)}, u32[]{:S(2)}) %copy-start.6) | copy-done | bytes 524312
  9.6 1.0 %copy-done.7 = bf16[512,512]{1,0:T(8,128)(2,1)S(1)} copy-done((bf16[512,512]{1,0:T(8,128)(2,1)S(1)}, bf16[512,512]{1,0:T(8,128)(2,1)}, u32[]{:S(2)}) %copy-start.7) | copy-done | bytes 524312
  10.7 0.9 %copy-done.8 = bf16[256,512]{1,0:T(8,128)(2,1)S(1)} copy-done((bf16[256,512]{1,0:T(8,128)(2,1)S(1)}, bf16[256,512]{1,0:T(8,128)(2,1)}, u32[]{:S(2)}) %copy-start.8) | copy-done | bytes 262168
  11.6 61.8 %encode_process.1 = bf16[32,512]{1,0:T(8,128)(2,1)S(1)} custom-call(bf16[256,512]{1,0:T(8,128)(2,1)S(1)} %copy-done.8, bf16[32,512]{1,0:T(8,128)(2,1)S(1)} %copy-done.9, s32[64,16]{1,0:T(8,128)S(1)} %copy.28.send_rows, s32[1,64]{1,0:T(1,128)S(1)} %bitcast.30, s32[1,512]{1,0:T(1,128)S(1)} %bitcast.16, s32[1,512]{1,0:T(1,128)S(1)} %bitcast.17, ...), custom_call_target="tpu_custom_call" | custom-call | tf_op jit(solution)/shard_map/encode_process/pallas_call | solution.py:241
  73.4 0.6 copy.30
  (9 shorter events, 0.0 us)
Async XLA Ops:
  0.0 0.7 copy-start.26
  0.0 0.9 %copy-start.9 = (bf16[32,512]{1,0:T(8,128)(2,1)S(1)}, bf16[32,512]{1,0:T(8,128)(2,1)}, u32[]{:S(2)}) copy-start(bf16[32,512]{1,0:T(8,128)(2,1)} %rows.1) | copy-start | bytes 98308
  0.7 0.7 copy-start.10
  0.7 0.7 copy-start.11
  0.7 0.7 copy-start.12
  0.7 0.7 copy-start.13
  0.7 0.7 copy-start.14
  0.7 0.7 %copy-start.15 = (f32[512]{0:T(512)S(1)}, f32[512]{0:T(512)}, u32[]{:S(2)}) copy-start(f32[512]{0:T(512)} %param.39) | copy-start | bytes 6148
  0.7 0.7 %copy-start.16 = (f32[512]{0:T(512)S(1)}, f32[512]{0:T(512)}, u32[]{:S(2)}) copy-start(f32[512]{0:T(512)} %param.41) | copy-start | bytes 6148
  0.7 0.8 %copy-start.17 = (f32[512]{0:T(512)S(1)}, f32[512]{0:T(512)}, u32[]{:S(2)}) copy-start(f32[512]{0:T(512)} %param.43) | copy-start | bytes 6148
  0.7 0.8 %copy-start.18 = (f32[512]{0:T(512)S(1)}, f32[512]{0:T(512)}, u32[]{:S(2)}) copy-start(f32[512]{0:T(512)} %param.44) | copy-start | bytes 6148
  0.8 0.8 %copy-start.19 = (f32[512]{0:T(512)S(1)}, f32[512]{0:T(512)}, u32[]{:S(2)}) copy-start(f32[512]{0:T(512)} %param.46) | copy-start | bytes 6148
  0.8 0.8 %copy-start.20 = (f32[512]{0:T(512)S(1)}, f32[512]{0:T(512)}, u32[]{:S(2)}) copy-start(f32[512]{0:T(512)} %param.48) | copy-start | bytes 6148
  0.8 0.8 %copy-start.21 = (f32[512]{0:T(512)S(1)}, f32[512]{0:T(512)}, u32[]{:S(2)}) copy-start(f32[512]{0:T(512)} %param.50) | copy-start | bytes 6148
  0.8 0.8 %copy-start.22 = (f32[512]{0:T(512)S(1)}, f32[512]{0:T(512)}, u32[]{:S(2)}) copy-start(f32[512]{0:T(512)} %param.52) | copy-start | bytes 6148
  0.8 0.8 %copy-start.23 = (f32[512]{0:T(512)S(1)}, f32[512]{0:T(512)}, u32[]{:S(2)}) copy-start(f32[512]{0:T(512)} %param.53) | copy-start | bytes 6148
  0.8 0.8 %copy-start.24 = (s32[64]{0:T(128)S(1)}, s32[64]{0:T(128)}, u32[]{:S(2)}) copy-start(s32[64]{0:T(128)} %param.30) | copy-start | bytes 772
  0.8 0.8 %copy-start.25 = (s32[32]{0:T(128)S(1)}, s32[32]{0:T(128)}, u32[]{:S(2)}) copy-start(s32[32]{0:T(128)} %param.33) | copy-start | bytes 388
  1.6 1.2 %copy-start = (bf16[1024,512]{1,0:T(8,128)(2,1)S(1)}, bf16[1024,512]{1,0:T(8,128)(2,1)}, u32[]{:S(2)}) copy-start(bf16[1024,512]{1,0:T(8,128)(2,1)} %rest_0_.1) | copy-start | bytes 3145732
  2.8 1.2 %copy-start.1 = (bf16[1024,512]{1,0:T(8,128)(2,1)S(1)}, bf16[1024,512]{1,0:T(8,128)(2,1)}, u32[]{:S(2)}) copy-start(bf16[1024,512]{1,0:T(8,128)(2,1)} %rest_2_.1) | copy-start | bytes 3145732
  4.0 1.2 %copy-start.2 = (bf16[1024,512]{1,0:T(8,128)(2,1)S(1)}, bf16[1024,512]{1,0:T(8,128)(2,1)}, u32[]{:S(2)}) copy-start(bf16[1024,512]{1,0:T(8,128)(2,1)} %rest_4_.1) | copy-start | bytes 3145732
  5.3 1.2 %copy-start.3 = (bf16[1024,512]{1,0:T(8,128)(2,1)S(1)}, bf16[1024,512]{1,0:T(8,128)(2,1)}, u32[]{:S(2)}) copy-start(bf16[1024,512]{1,0:T(8,128)(2,1)} %rest_6_.1) | copy-start | bytes 3145732
  6.5 1.0 %copy-start.4 = (bf16[512,512]{1,0:T(8,128)(2,1)S(1)}, bf16[512,512]{1,0:T(8,128)(2,1)}, u32[]{:S(2)}) copy-start(bf16[512,512]{1,0:T(8,128)(2,1)} %rest_1_.1) | copy-start | bytes 1572868
  7.5 1.0 %copy-start.5 = (bf16[512,512]{1,0:T(8,128)(2,1)S(1)}, bf16[512,512]{1,0:T(8,128)(2,1)}, u32[]{:S(2)}) copy-start(bf16[512,512]{1,0:T(8,128)(2,1)} %rest_3_.1) | copy-start | bytes 1572868
  8.6 1.0 %copy-start.6 = (bf16[512,512]{1,0:T(8,128)(2,1)S(1)}, bf16[512,512]{1,0:T(8,128)(2,1)}, u32[]{:S(2)}) copy-start(bf16[512,512]{1,0:T(8,128)(2,1)} %rest_5_.1) | copy-start | bytes 1572868
  9.6 1.0 %copy-start.7 = (bf16[512,512]{1,0:T(8,128)(2,1)S(1)}, bf16[512,512]{1,0:T(8,128)(2,1)}, u32[]{:S(2)}) copy-start(bf16[512,512]{1,0:T(8,128)(2,1)} %rest_7_.1) | copy-start | bytes 1572868
  10.7 0.9 %copy-start.8 = (bf16[256,512]{1,0:T(8,128)(2,1)S(1)}, bf16[256,512]{1,0:T(8,128)(2,1)}, u32[]{:S(2)}) copy-start(bf16[256,512]{1,0:T(8,128)(2,1)} %grid.1) | copy-start | bytes 786436

commit v2 on v1

--- a/solution.py
+++ b/solution.py
@@ -14,7 +14,7 @@
 I32 = jnp.int32
 CAP = 16
 MOVE = 8
-WEIGHTS = 8
+ARGS = 27
 
 
 def iota(shape, dim):
@@ -60,15 +60,15 @@
 
 def kernel(
     bands, zs, ys, order,
-    grid, rows, send_rows, send_count, enc_s, enc_r, move_to, proc_s, proc_r,
-    e_b1, e_b2, en_b1, en_b2, e_gain, p_b1, p_b2, pn_b1, pn_b2, p_gain,
-    *rest,
+    *refs,
 ):
-    hbm, out = rest[:WEIGHTS], rest[WEIGHTS]
-    held = rest[WEIGHTS + 1 : 2 * WEIGHTS + 1]
+    hbm, out = refs[:ARGS], refs[ARGS]
+    held = refs[ARGS + 1 : 2 * ARGS + 1]
     (send, recv, pick, base, total, meta_out, meta_in, move_out, move_in,
-     w_sem, ss, rs, ms, mr, vs, vr) = rest[2 * WEIGHTS + 1 :]
-    e_w1, e_w2, n_w1, n_w2, p_w1, p_w2, q_w1, q_w2 = held
+     in_sem, ss, rs, ms, mr, vs, vr) = refs[2 * ARGS + 1 :]
+    (send_rows, send_count, grid, move_to, enc_s, rows, enc_r, proc_s, proc_r,
+     e_w1, e_b1, n_w1, en_b1, e_w2, e_b2, n_w2, en_b2, e_gain,
+     p_w1, p_b1, p_w2, p_b2, q_w1, pn_b1, q_w2, pn_b2, p_gain) = held
     doms = zs * ys
     width = grid.shape[1]
     count = rows.shape[0]
@@ -86,9 +86,11 @@
     for k in range(1, bands):
         pl.semaphore_signal(barrier, inc=1, device_id=((band + k) % bands, dom), device_id_type=MESH)
 
-    loads = [pltpu.make_async_copy(hbm[i], held[i], w_sem.at[i]) for i in range(WEIGHTS)]
+    loads = [pltpu.make_async_copy(hbm[i], held[i], in_sem.at[i]) for i in range(ARGS)]
     for load in loads:
         load.start()
+    for load in loads[:3]:
+        load.wait()
 
     block = min(256, slots)
     listed = send_rows[...].astype(F32).astype(BF16)
@@ -99,7 +101,7 @@
         rel = slot // CAP
         there = ((z + rel // ys) % zs) * ys + (y + rel % ys) % ys
         peer = there == iota((block, doms), 1)
-        mine = dot(one_hot(peer), listed)
+        mine = lax.dot_general(one_hot(peer), listed, (((1,), (1,)), ((), ())), preferred_element_type=F32)
         lane = (iota((block, CAP), 0) % CAP) == iota((block, CAP), 1)
         index = dot(jnp.where(lane, mine, 0.0).astype(BF16), jnp.ones((CAP, grid.shape[0]), BF16))
         limit = dot(jnp.where(peer, counts, 0.0).astype(BF16), jnp.ones((doms, grid.shape[0]), BF16))
@@ -110,6 +112,8 @@
 
     lax.fori_loop(0, slots // block, gather, 0)
 
+    for load in loads[3:9]:
+        load.wait()
     dest = move_to[...]
     leaves = (dest // count) != band
     before = one_hot(iota((count, count), 0) < iota((count, count), 1))
@@ -148,11 +152,11 @@
     receiver = lanes_to_rows(enc_r[...])
     recv_hot = one_hot(((lane % count) == receiver) & (lane < 2 * count))
     hot_t = one_hot(iota((count, edges), 0) == enc_r[...])
-    loads[0].wait()
+    for load in loads[9:]:
+        load.wait()
     recv_proj = dot(rows[...], e_w1[width:]) + e_b1[...]
     stack = jnp.concatenate([halves(recv_proj), jnp.zeros((128 - 2 * count, recv_proj.shape[1]), BF16)], axis=0)
     base[...] = dot(recv_hot, stack)
-    loads[2].wait()
     node_pre = dot(rows[...], n_w1[:width]) + en_b1[...]
     proc_send, proc_recv = lanes_to_rows(proc_s[...]), lanes_to_rows(proc_r[...])
     proc_hot = one_hot((lane % count) == jnp.where((lane // count) % 2 == 0, proc_send, proc_recv))
@@ -168,8 +172,6 @@
     lands = moved[:count] == iota((count, bands * 2 * MOVE), 0) + band * count
     left = (iota((count, bands * 2 * MOVE), 1) % (2 * MOVE)) < MOVE
     place_in = jnp.concatenate([one_hot(lands & left), one_hot(lands & jnp.logical_not(left))], axis=0)
-    for i in (1, 3, 4, 5, 6, 7):
-        loads[i].wait()
 
     span = per * CAP
     for i in range(chunks):
@@ -230,20 +232,24 @@
         count, width = mesh_latent.shape
         edges = enc_sender.shape[0]
         slots = doms * CAP
-        weights = (enc_edge_w1, enc_edge_w2, enc_node_w1, enc_node_w2, proc_edge_w1, proc_edge_w2, proc_node_w1, proc_node_w2)
-        small = (send_count, enc_sender, enc_receiver, move_to, proc_sender, proc_receiver,
-                 enc_edge_b1, enc_edge_b2, enc_node_b1, enc_node_b2, enc_gain,
-                 proc_edge_b1, proc_edge_b2, proc_node_b1, proc_node_b2, proc_gain)
-        small = [a.reshape(1, -1) for a in small]
+        row = lambda a: a.reshape(1, -1)
+        operands = (
+            send_rows.T, row(send_count), grid_latent, row(move_to), row(enc_sender), mesh_latent, row(enc_receiver),
+            row(proc_sender), row(proc_receiver),
+            enc_edge_w1, row(enc_edge_b1), enc_node_w1, row(enc_node_b1), enc_edge_w2, row(enc_edge_b2),
+            enc_node_w2, row(enc_node_b2), row(enc_gain),
+            proc_edge_w1, row(proc_edge_b1), proc_edge_w2, row(proc_edge_b2), proc_node_w1, row(proc_node_b1),
+            proc_node_w2, row(proc_node_b2), row(proc_gain),
+        )
         vmem = pl.BlockSpec(memory_space=pltpu.VMEM)
         dma = pltpu.SemaphoreType.DMA
         chunks = max(1, slots // 256)
         return pl.pallas_call(
             functools.partial(kernel, bands, zs, ys, order),
             out_shape=jax.ShapeDtypeStruct((count, width), BF16),
-            in_specs=[vmem] * (3 + len(small)) + [pl.BlockSpec(memory_space=pl.ANY)] * WEIGHTS,
+            in_specs=[pl.BlockSpec(memory_space=pltpu.HBM)] * ARGS,
             out_specs=vmem,
-            scratch_shapes=[pltpu.VMEM(w.shape, w.dtype) for w in weights] + [
+            scratch_shapes=[pltpu.VMEM(w.shape, w.dtype) for w in operands] + [
                 pltpu.VMEM((slots, width), BF16),
                 pltpu.VMEM((slots, width), BF16),
                 pltpu.VMEM((edges, slots), BF16),
@@ -253,13 +259,13 @@
                 pltpu.VMEM((bands, 2 * MOVE, 128), I32),
                 pltpu.VMEM((2 * MOVE, width // 2), BF16),
                 pltpu.VMEM((bands, 2 * MOVE, width // 2), BF16),
-                dma((WEIGHTS,)), dma((1,)), dma((chunks,)), dma((1,)), dma((1,)), dma((1,)), dma((1,)),
+                dma((ARGS,)), dma((1,)), dma((chunks,)), dma((1,)), dma((1,)), dma((1,)), dma((1,)),
             ],
             compiler_params=pltpu.CompilerParams(
-                collective_id=0, has_side_effects=True, vmem_limit_bytes=40 * 1024 * 1024
+                collective_id=0, has_side_effects=True, vmem_limit_bytes=63 * 1024 * 1024
             ),
             name="encode_process",
-        )(grid_latent, mesh_latent, send_rows, *small, *weights)
+        )(*operands)
 
     split, whole = P(("band", "dom")), P()
     return jax.shard_map(

time: 74.6 us -> 64.1 us (0.86)
  local copies, waits for them, and re-layouts: 12.1 us -> 1.38 us
    unnamed x56 -> x1, local copies, waits for them, and re-layouts: 12.1 us -> 1.38 us
    pallas_call x1, Pallas kernels: 61.8 us -> 62.5 us  [shards(): pl.pallas_call(functools.partial(kernel, bands, zs, ys, order), out_shape...]
where the time goes in v2:
time: 64.1 us; the launch traced here: 63.9 us
  Pallas kernels  62.5 us (98%)
  local copies, waits for them, and re-layouts  1.38 us (2%)
    pallas_call x1, Pallas kernels, shards(): pl.pallas_call(functools.partial(kernel, bands, zs, ys, order), out_shape...  62.5 us
    unnamed x1, local copies, waits for them, and re-layouts  1.38 us

profile of v2, /device:TPU:1, one launch (start us, length us, event | category | flops | bytes accessed | tf_op | source)
XLA Modules:
  0.0 63.9 jit_solution(3879555019316841488)
XLA Ops:
  0.0 62.5 %encode_process.1 = bf16[32,512]{1,0:T(8,128)(2,1)} custom-call(s32[16,64]{1,0:T(8,128)} %bitcast.17, s32[1,64]{1,0:T(1,128)} %bitcast.32, bf16[256,512]{1,0:T(8,128)(2,1)} %refs_2_.1, s32[1,32]{1,0:T(1,128)} %bitcast.33, s32[1,512]{1,0:T(1,128)} %bitcast.18, bf16[32,512]{1,0:T(8,128)(2,1)} %refs_5_.1, s32[1,512]{1,0:T(1,128)} %bitcast.19, ...), custom_call_target="tpu_custom_call" | custom-call | tf_op jit(solution)/shard_map/encode_process/pallas_call | solution.py:247
  62.5 1.4 %copy.29 = bf16[32,512]{1,0:T(8,128)(2,1)} copy(bf16[32,512]{1,0:T(8,128)(2,1)} %encode_process.1) | data formatting | bytes 65536

commit v3 on v2

--- a/solution.py
+++ b/solution.py
@@ -14,7 +14,7 @@
 I32 = jnp.int32
 CAP = 16
 MOVE = 8
-ARGS = 27
+ARGS = 28
 
 
 def iota(shape, dim):
@@ -30,7 +30,8 @@
 
 
 def silu(v):
-    return v / (1.0 + jnp.exp(-v))
+    half = 0.5 * v
+    return half + half * jnp.tanh(half)
 
 
 def halves(v):
@@ -56,6 +57,19 @@
 
 def lanes_to_rows(row):
     return jnp.broadcast_to(row, (128, row.shape[1])).T
+
+
+def far_order(zs, ys):
+    hops = lambda v, n: min(v, n - v)
+    far = lambda o: hops(o[0], zs) + hops(o[1], ys)
+    opposite = lambda o: (-o[0] % zs, -o[1] % ys)
+    order = []
+    for o in sorted(((a, c) for a in range(zs) for c in range(ys)), key=far, reverse=True):
+        swapped = (o[1] % zs, o[0] % ys)
+        for q in (o, swapped, opposite(o), opposite(swapped)):
+            if q not in order and q != (0, 0) and far(q) == far(o):
+                order.append(q)
+    return order
 
 
 def kernel(
@@ -66,7 +80,7 @@
     held = refs[ARGS + 1 : 2 * ARGS + 1]
     (send, recv, pick, base, total, meta_out, meta_in, move_out, move_in,
      in_sem, ss, rs, ms, mr, vs, vr) = refs[2 * ARGS + 1 :]
-    (send_rows, send_count, grid, move_to, enc_s, rows, enc_r, proc_s, proc_r,
+    (send_rows, send_count, grid, turns, move_to, enc_s, rows, enc_r, proc_s, proc_r,
      e_w1, e_b1, n_w1, en_b1, e_w2, e_b2, n_w2, en_b2, e_gain,
      p_w1, p_b1, p_w2, p_b2, q_w1, pn_b1, q_w2, pn_b2, p_gain) = held
     doms = zs * ys
@@ -79,40 +93,56 @@
     band, dom = lax.axis_index("band"), lax.axis_index("dom")
     z, y = dom // ys, dom % ys
 
+    sign = 1 - 2 * (band % 2)
+    far_bands = sorted(range(1, bands), key=lambda k: -min(k, bands - k))
+
+    def peer_at(a, c):
+        return ((z + sign * a + zs) % zs) * ys + (y + sign * c + ys) % ys
+
+    def turn(to_z, to_y):
+        rel = ((sign * to_z) % zs) * ys + (sign * to_y) % ys
+        hot = iota((doms, rel.shape[1]), 0) == rel
+        return jnp.sum(jnp.where(hot, turns[:, :1], 0), axis=0, keepdims=True)
+
+    loads = [pltpu.make_async_copy(hbm[i], held[i], in_sem.at[i]) for i in range(ARGS)]
+    for load in loads[:4]:
+        load.start()
+
     barrier = pltpu.get_barrier_semaphore()
     for a, c in order:
-        there = ((z + a) % zs) * ys + (y + c) % ys
-        pl.semaphore_signal(barrier, inc=1, device_id=(band, there), device_id_type=MESH)
-    for k in range(1, bands):
+        pl.semaphore_signal(barrier, inc=1, device_id=(band, peer_at(a, c)), device_id_type=MESH)
+    for k in far_bands:
         pl.semaphore_signal(barrier, inc=1, device_id=((band + k) % bands, dom), device_id_type=MESH)
-
-    loads = [pltpu.make_async_copy(hbm[i], held[i], in_sem.at[i]) for i in range(ARGS)]
-    for load in loads:
-        load.start()
-    for load in loads[:3]:
+    for load in loads[:4]:
         load.wait()
 
-    block = min(256, slots)
+    span = per * CAP
+    points = grid.shape[0]
     listed = send_rows[...].astype(F32).astype(BF16)
     counts = send_count[...].astype(F32)
-
-    def gather(i, carry):
-        slot = iota((block, doms), 0) + i * block
-        rel = slot // CAP
-        there = ((z + rel // ys) % zs) * ys + (y + rel % ys) % ys
-        peer = there == iota((block, doms), 1)
+    peers = iota((1, doms), 1)
+    at_turn = turn(peers // ys - z, peers % ys - y)
+    for i in range(chunks):
+        peer = at_turn == iota((span, doms), 0) // CAP + i * per
         mine = lax.dot_general(one_hot(peer), listed, (((1,), (1,)), ((), ())), preferred_element_type=F32)
-        lane = (iota((block, CAP), 0) % CAP) == iota((block, CAP), 1)
-        index = dot(jnp.where(lane, mine, 0.0).astype(BF16), jnp.ones((CAP, grid.shape[0]), BF16))
-        limit = dot(jnp.where(peer, counts, 0.0).astype(BF16), jnp.ones((doms, grid.shape[0]), BF16))
-        at = iota((block, grid.shape[0]), 0) % CAP
-        hot = (index == iota((block, grid.shape[0]), 1).astype(F32)) & (at.astype(F32) < limit)
-        send[pl.ds(pl.multiple_of(i * block, block), block), :] = dot(one_hot(hot), grid[...]).astype(BF16)
-        return carry
-
-    lax.fori_loop(0, slots // block, gather, 0)
-
-    for load in loads[3:9]:
+        lane = (iota((span, CAP), 0) % CAP) == iota((span, CAP), 1)
+        index = dot(jnp.where(lane, mine, 0.0).astype(BF16), jnp.ones((CAP, points), BF16))
+        limit = dot(jnp.where(peer, counts, 0.0).astype(BF16), jnp.ones((doms, points), BF16))
+        at = iota((span, points), 0) % CAP
+        hot = (index == iota((span, points), 1).astype(F32)) & (at.astype(F32) < limit)
+        send[pl.ds(i * span, span), :] = dot(one_hot(hot), grid[...]).astype(BF16)
+        if i == 0:
+            pl.semaphore_wait(barrier, len(order) + bands - 1)
+        for t in range(max(1, i * per), (i + 1) * per):
+            pltpu.make_async_remote_copy(
+                send.at[pl.ds(t * CAP, CAP)], recv.at[pl.ds(t * CAP, CAP)], ss.at[0], rs.at[i],
+                device_id=(band, peer_at(*order[t - 1])), device_id_type=MESH,
+            ).start()
+    for load in loads[4:]:
+        load.start()
+    recv[pl.ds(0, CAP), :] = send[pl.ds(0, CAP), :]
+
+    for load in loads[4:10]:
         load.wait()
     dest = move_to[...]
     leaves = (dest // count) != band
@@ -124,35 +154,22 @@
     meta_out[...] = jnp.concatenate([goes, goes], axis=0)
     meta_in[0] = jnp.full((2 * MOVE, 128), -1, I32)
     move_in[0] = jnp.zeros((2 * MOVE, width // 2), BF16)
-
-    pl.semaphore_wait(barrier, len(order) + bands - 1)
-
-    for a, c in order:
-        there = ((z + a) % zs) * ys + (y + c) % ys
-        at = (a * ys + c) * CAP
-        pltpu.make_async_remote_copy(
-            send.at[pl.ds(at, CAP)], recv.at[pl.ds(at, CAP)], ss.at[0], rs.at[(a * ys + c) // per],
-            device_id=(band, there), device_id_type=MESH,
-        ).start()
-    for k in range(1, bands):
+    for k in far_bands:
         pltpu.make_async_remote_copy(
             meta_out, meta_in.at[k], ms.at[0], mr.at[0],
             device_id=((band + k) % bands, dom), device_id_type=MESH,
         ).start()
-    recv[pl.ds(0, CAP), :] = send[pl.ds(0, CAP), :]
 
     sender = enc_s[...]
     from_dom = sender // CAP
-    rel_z = (z - from_dom // ys + zs) % zs
-    rel_y = (y - from_dom % ys + ys) % ys
-    place = lanes_to_rows((rel_z * ys + rel_y) * CAP + sender % CAP)
+    place = lanes_to_rows(turn(z - from_dom // ys, y - from_dom % ys) * CAP + sender % CAP)
     for i in range(slots // 128):
         pick[:, pl.ds(i * 128, 128)] = one_hot(place == iota((edges, 128), 1) + i * 128)
     lane = iota((edges, 128), 1)
     receiver = lanes_to_rows(enc_r[...])
     recv_hot = one_hot(((lane % count) == receiver) & (lane < 2 * count))
     hot_t = one_hot(iota((count, edges), 0) == enc_r[...])
-    for load in loads[9:]:
+    for load in loads[10:]:
         load.wait()
     recv_proj = dot(rows[...], e_w1[width:]) + e_b1[...]
     stack = jnp.concatenate([halves(recv_proj), jnp.zeros((128 - 2 * count, recv_proj.shape[1]), BF16)], axis=0)
@@ -173,7 +190,6 @@
     left = (iota((count, bands * 2 * MOVE), 1) % (2 * MOVE)) < MOVE
     place_in = jnp.concatenate([one_hot(lands & left), one_hot(lands & jnp.logical_not(left))], axis=0)
 
-    span = per * CAP
     for i in range(chunks):
         first = 1 if i == 0 else i * per
         blocks = per - 1 if i == 0 else per
@@ -193,7 +209,7 @@
 
     packed = dot(pack, mesh_enc)
     move_out[...] = jnp.concatenate([packed[:, : width // 2], packed[:, width // 2 :]], axis=0).astype(BF16)
-    for k in range(1, bands):
+    for k in far_bands:
         pltpu.make_async_remote_copy(
             move_out, move_in.at[k], vs.at[0], vr.at[0],
             device_id=((band + k) % bands, dom), device_id_type=MESH,
@@ -221,8 +237,10 @@
     bands, doms = mesh.shape["band"], mesh.shape["dom"]
     zs = 2 ** ((doms.bit_length() - 1) // 2)
     ys = doms // zs
-    offsets = [(a, c) for a in range(zs) for c in range(ys) if (a, c) != (0, 0)]
-    order = [offsets[i] for i in np.random.RandomState(0).permutation(len(offsets))]
+    order = far_order(zs, ys)
+    turns = np.zeros((doms, 128), np.int32)
+    for t, (a, c) in enumerate(order):
+        turns[a * ys + c] = t + 1
 
     def shards(
         grid_latent, mesh_latent, send_rows, send_count, enc_sender, enc_receiver, move_to, proc_sender, proc_receiver,
@@ -234,7 +252,7 @@
         slots = doms * CAP
         row = lambda a: a.reshape(1, -1)
         operands = (
-            send_rows.T, row(send_count), grid_latent, row(move_to), row(enc_sender), mesh_latent, row(enc_receiver),
+            send_rows.T, row(send_count), grid_latent, jnp.asarray(turns), row(move_to), row(enc_sender), mesh_latent, row(enc_receiver),
             row(proc_sender), row(proc_receiver),
             enc_edge_w1, row(enc_edge_b1), enc_node_w1, row(enc_node_b1), enc_edge_w2, row(enc_edge_b2),
             enc_node_w2, row(enc_node_b2), row(enc_gain),

time: 64.1 us -> 62.9 us (0.981)
  Pallas kernels: 62.5 us -> 61.3 us
    pallas_call x1, Pallas kernels: 62.5 us -> 61.3 us  [shards(): pl.pallas_call(functools.partial(kernel, bands, zs, ys, order), out_shape...]
where the time goes in v3:
time: 62.9 us; the launch traced here: 62.6 us
  Pallas kernels  61.3 us (97%)
  local copies, waits for them, and re-layouts  1.38 us (2%)
    pallas_call x1, Pallas kernels, shards(): pl.pallas_call(functools.partial(kernel, bands, zs, ys, order), out_shape...  61.3 us
    unnamed x1, local copies, waits for them, and re-layouts  1.38 us

profile of v3, /device:TPU:1, one launch (start us, length us, event | category | flops | bytes accessed | tf_op | source)
XLA Modules:
  0.0 62.6 jit_solution(9249489700666849327)
XLA Ops:
  0.0 61.3 %encode_process.1 = bf16[32,512]{1,0:T(8,128)(2,1)} custom-call(s32[16,64]{1,0:T(8,128)} %bitcast.17, s32[1,64]{1,0:T(1,128)} %bitcast.32, bf16[256,512]{1,0:T(8,128)(2,1)} %refs_2_.1, s32[64,128]{1,0:T(8,128)} %constant.2.clone.refs_3_, s32[1,32]{1,0:T(1,128)} %bitcast.33, s32[1,512]{1,0:T(1,128)} %bitcast.18, bf16[32,512]{1,0:T(8,128)(2,1)} %refs_6_.1, ...), custom_call_target="tpu_custom_call" | custom-call | tf_op jit(solution)/shard_map/encode_process/pallas_call | solution.py:265
  61.3 1.4 %copy.30 = bf16[32,512]{1,0:T(8,128)(2,1)} copy(bf16[32,512]{1,0:T(8,128)(2,1)} %encode_process.1) | data formatting | bytes 65536

commit v4 on v3

--- a/solution.py
+++ b/solution.py
@@ -39,20 +39,29 @@
     return jnp.concatenate([high, (v - high.astype(F32)).astype(BF16)], axis=0)
 
 
-def node_out(rows, pre, agg, w1, w2, b2, gain):
-    width = rows.shape[1]
-    z = silu(pre + dot(agg, w1[width:])).astype(BF16)
+def node_out(rows, pre, w2, b2, gain):
+    z = silu(pre).astype(BF16)
     u = dot(z, w2[...]) + b2
     center = u - jnp.mean(u, axis=-1, keepdims=True)
     spread = jnp.mean(center * center, axis=-1, keepdims=True)
     return (rows.astype(F32) + gain * (center * lax.rsqrt(spread + 1e-05))).astype(BF16)
 
 
-def aggregate(hidden, hot_t, w2, b2):
-    rows = hot_t.shape[0]
-    two = dot(halves(dot(hot_t, hidden)), w2[...])
+def fold(w2, b2, hot_t, w1, both):
+    width, columns = w2.shape[1], w1.shape[1]
+    product = dot(w2[...], w1[width:])
+    high = product.astype(BF16)
+    both[:, :columns] = high
+    both[:, columns:] = (product - high.astype(F32)).astype(BF16)
+    bias = dot(halves(jnp.broadcast_to(b2, (8, width))), w1[width:])
     count = jnp.sum(hot_t.astype(F32), axis=1, keepdims=True)
-    return (two[:rows] + two[rows:] + count * b2).astype(BF16)
+    return count * (bias[:1] + bias[8:9])
+
+
+def edge_part(hidden_sum, both):
+    rows, columns = hidden_sum.shape[0], both.shape[1] // 2
+    two = dot(halves(hidden_sum), both[...])
+    return two[:rows, :columns] + (two[rows:, :columns] + two[:rows, columns:])
 
 
 def lanes_to_rows(row):
@@ -64,7 +73,7 @@
     far = lambda o: hops(o[0], zs) + hops(o[1], ys)
     opposite = lambda o: (-o[0] % zs, -o[1] % ys)
     order = []
-    for o in sorted(((a, c) for a in range(zs) for c in range(ys)), key=far, reverse=True):
+    for o in sorted(((a, c) for a in range(zs) for c in range(ys)), key=lambda o: (-max(hops(o[0], zs), hops(o[1], ys)), -far(o))):
         swapped = (o[1] % zs, o[0] % ys)
         for q in (o, swapped, opposite(o), opposite(swapped)):
             if q not in order and q != (0, 0) and far(q) == far(o):
@@ -78,7 +87,7 @@
 ):
     hbm, out = refs[:ARGS], refs[ARGS]
     held = refs[ARGS + 1 : 2 * ARGS + 1]
-    (send, recv, pick, base, total, meta_out, meta_in, move_out, move_in,
+    (send, recv, pick, base, e_both, p_both, meta_out, meta_in, move_out, move_in,
      in_sem, ss, rs, ms, mr, vs, vr) = refs[2 * ARGS + 1 :]
     (send_rows, send_count, grid, turns, move_to, enc_s, rows, enc_r, proc_s, proc_r,
      e_w1, e_b1, n_w1, en_b1, e_w2, e_b2, n_w2, en_b2, e_gain,
@@ -174,10 +183,11 @@
     recv_proj = dot(rows[...], e_w1[width:]) + e_b1[...]
     stack = jnp.concatenate([halves(recv_proj), jnp.zeros((128 - 2 * count, recv_proj.shape[1]), BF16)], axis=0)
     base[...] = dot(recv_hot, stack)
-    node_pre = dot(rows[...], n_w1[:width]) + en_b1[...]
+    node_pre = dot(rows[...], n_w1[:width]) + en_b1[...] + fold(e_w2, e_b2[...], hot_t, n_w1, e_both)
     proc_send, proc_recv = lanes_to_rows(proc_s[...]), lanes_to_rows(proc_r[...])
     proc_hot = one_hot((lane % count) == jnp.where((lane // count) % 2 == 0, proc_send, proc_recv))
     proc_hot_t = one_hot(iota((count, edges), 0) == proc_r[...])
+    proc_bias = fold(p_w2, p_b2[...], proc_hot_t, q_w1, p_both) + pn_b1[...]
     pack = one_hot(packs)
     stays = one_hot(dest - band * count == iota((count, count), 0))
     pltpu.make_async_remote_copy(
@@ -197,15 +207,15 @@
         pltpu.make_async_remote_copy(
             landed, landed, ss.at[0], rs.at[i], device_id=(band, (z * ys + (y + 1) % ys)), device_id_type=MESH
         ).wait_recv()
-        part = dot(pick[:, pl.ds(i * span, span)], recv[pl.ds(i * span, span), :])
-        if i == 0:
-            total[...] = part
-        elif i < chunks - 1:
-            total[...] += part
-    gathered = (total[...] + part).astype(BF16) if chunks > 1 else part.astype(BF16)
-    hidden = silu(base[...] + dot(gathered, e_w1[:width])).astype(BF16)
-    agg = aggregate(hidden, hot_t, e_w2, e_b2[...])
-    mesh_enc = node_out(rows[...], node_pre, agg, n_w1, n_w2, en_b2[...], e_gain[...])
+        parts = []
+        for e in range(0, edges, 512):
+            got = dot(pick[pl.ds(e, 512), pl.ds(i * span, span)], recv[pl.ds(i * span, span), :]).astype(BF16)
+            pre = base[pl.ds(e, 512), :] + dot(got, e_w1[:width])
+            if i < chunks - 1:
+                base[pl.ds(e, 512), :] = pre
+            else:
+                parts.append(dot(hot_t[:, e : e + 512], silu(pre).astype(BF16)))
+    mesh_enc = node_out(rows[...], node_pre + edge_part(sum(parts), e_both), n_w2, en_b2[...], e_gain[...])
 
     packed = dot(pack, mesh_enc)
     move_out[...] = jnp.concatenate([packed[:, : width // 2], packed[:, width // 2 :]], axis=0).astype(BF16)
@@ -223,10 +233,13 @@
     proc_in = (kept + jnp.concatenate([came[:count], came[count:]], axis=1)).astype(BF16)
 
     projected = jnp.concatenate([dot(proc_in, p_w1[:width]), dot(proc_in, p_w1[width:]) + p_b1[...]], axis=0)
-    hidden = silu(dot(proc_hot, halves(projected))).astype(BF16)
-    node_pre = dot(proc_in, q_w1[:width]) + pn_b1[...]
-    agg = aggregate(hidden, proc_hot_t, p_w2, p_b2[...])
-    out[...] = node_out(proc_in, node_pre, agg, q_w1, q_w2, pn_b2[...], p_gain[...])
+    stack = halves(projected)
+    node_pre = dot(proc_in, q_w1[:width]) + proc_bias
+    parts = []
+    for e in range(0, edges, 512):
+        hidden = silu(dot(proc_hot[e : e + 512], stack)).astype(BF16)
+        parts.append(dot(proc_hot_t[:, e : e + 512], hidden))
+    out[...] = node_out(proc_in, node_pre + edge_part(sum(parts), p_both), q_w2, pn_b2[...], p_gain[...])
     outgoing = send.at[pl.ds(CAP, slots - CAP)]
     pltpu.make_async_remote_copy(
         outgoing, outgoing, ss.at[0], rs.at[0], device_id=(band, (z * ys + (y + 1) % ys)), device_id_type=MESH
@@ -272,7 +285,8 @@
                 pltpu.VMEM((slots, width), BF16),
                 pltpu.VMEM((edges, slots), BF16),
                 pltpu.VMEM((edges, enc_edge_w1.shape[1]), F32),
-                pltpu.VMEM((edges, width), F32),
+                pltpu.VMEM((enc_edge_w2.shape[0], 2 * enc_node_w1.shape[1]), BF16),
+                pltpu.VMEM((proc_edge_w2.shape[0], 2 * proc_node_w1.shape[1]), BF16),
                 pltpu.VMEM((2 * MOVE, 128), I32),
                 pltpu.VMEM((bands, 2 * MOVE, 128), I32),
                 pltpu.VMEM((2 * MOVE, width // 2), BF16),

time: 62.9 us -> 62.5 us (level)
  no operation moved by 1% of the time
where the time goes in v4:
time: 62.5 us; the launch traced here: 62.3 us
  Pallas kernels  60.9 us (97%)
  local copies, waits for them, and re-layouts  1.38 us (2%)
    pallas_call x1, Pallas kernels, shards(): pl.pallas_call(functools.partial(kernel, bands, zs, ys, order), out_shape...  60.9 us
    unnamed x1, local copies, waits for them, and re-layouts  1.38 us

profile of v4, /device:TPU:1, one launch (start us, length us, event | category | flops | bytes accessed | tf_op | source)
XLA Modules:
  0.0 62.3 jit_solution(2512291512539668834)
XLA Ops:
  0.0 60.9 %encode_process.1 = bf16[32,512]{1,0:T(8,128)(2,1)} custom-call(s32[16,64]{1,0:T(8,128)} %bitcast.17, s32[1,64]{1,0:T(1,128)} %bitcast.32, bf16[256,512]{1,0:T(8,128)(2,1)} %refs_2_.1, s32[64,128]{1,0:T(8,128)} %constant.2.clone.refs_3_, s32[1,32]{1,0:T(1,128)} %bitcast.33, s32[1,512]{1,0:T(1,128)} %bitcast.18, bf16[32,512]{1,0:T(8,128)(2,1)} %refs_6_.1, ...), custom_call_target="tpu_custom_call" | custom-call | tf_op jit(solution)/shard_map/encode_process/pallas_call | solution.py:278
  60.9 1.4 %copy.30 = bf16[32,512]{1,0:T(8,128)(2,1)} copy(bf16[32,512]{1,0:T(8,128)(2,1)} %encode_process.1) | data formatting | bytes 65536

commit v5 on v4

--- a/solution.py
+++ b/solution.py
@@ -97,7 +97,9 @@
     count = rows.shape[0]
     edges = enc_s.shape[1]
     slots = doms * CAP
-    chunks = rs.shape[0]
+    halves_in = rs.shape[0]
+    group = doms // halves_in
+    chunks = max(1, slots // 256)
     per = doms // chunks
     band, dom = lax.axis_index("band"), lax.axis_index("dom")
     z, y = dom // ys, dom % ys
@@ -144,7 +146,7 @@
             pl.semaphore_wait(barrier, len(order) + bands - 1)
         for t in range(max(1, i * per), (i + 1) * per):
             pltpu.make_async_remote_copy(
-                send.at[pl.ds(t * CAP, CAP)], recv.at[pl.ds(t * CAP, CAP)], ss.at[0], rs.at[i],
+                send.at[pl.ds(t * CAP, CAP)], recv.at[pl.ds(t * CAP, CAP)], ss.at[0], rs.at[t // group],
                 device_id=(band, peer_at(*order[t - 1])), device_id_type=MESH,
             ).start()
     for load in loads[4:]:
@@ -200,18 +202,18 @@
     left = (iota((count, bands * 2 * MOVE), 1) % (2 * MOVE)) < MOVE
     place_in = jnp.concatenate([one_hot(lands & left), one_hot(lands & jnp.logical_not(left))], axis=0)
 
-    for i in range(chunks):
-        first = 1 if i == 0 else i * per
-        blocks = per - 1 if i == 0 else per
+    for i in range(halves_in):
+        first = 1 if i == 0 else i * group
+        blocks = group - 1 if i == 0 else group
         landed = recv.at[pl.ds(first * CAP, blocks * CAP)]
         pltpu.make_async_remote_copy(
             landed, landed, ss.at[0], rs.at[i], device_id=(band, (z * ys + (y + 1) % ys)), device_id_type=MESH
         ).wait_recv()
         parts = []
         for e in range(0, edges, 512):
-            got = dot(pick[pl.ds(e, 512), pl.ds(i * span, span)], recv[pl.ds(i * span, span), :]).astype(BF16)
+            got = dot(pick[pl.ds(e, 512), pl.ds(i * group * CAP, group * CAP)], recv[pl.ds(i * group * CAP, group * CAP), :]).astype(BF16)
             pre = base[pl.ds(e, 512), :] + dot(got, e_w1[:width])
-            if i < chunks - 1:
+            if i < halves_in - 1:
                 base[pl.ds(e, 512), :] = pre
             else:
                 parts.append(dot(hot_t[:, e : e + 512], silu(pre).astype(BF16)))
@@ -274,7 +276,6 @@
         )
         vmem = pl.BlockSpec(memory_space=pltpu.VMEM)
         dma = pltpu.SemaphoreType.DMA
-        chunks = max(1, slots // 256)
         return pl.pallas_call(
             functools.partial(kernel, bands, zs, ys, order),
             out_shape=jax.ShapeDtypeStruct((count, width), BF16),
@@ -291,7 +292,7 @@
                 pltpu.VMEM((bands, 2 * MOVE, 128), I32),
                 pltpu.VMEM((2 * MOVE, width // 2), BF16),
                 pltpu.VMEM((bands, 2 * MOVE, width // 2), BF16),
-                dma((ARGS,)), dma((1,)), dma((chunks,)), dma((1,)), dma((1,)), dma((1,)), dma((1,)),
+                dma((ARGS,)), dma((1,)), dma((2,)), dma((1,)), dma((1,)), dma((1,)), dma((1,)),
             ],
             compiler_params=pltpu.CompilerParams(
                 collective_id=0, has_side_effects=True, vmem_limit_bytes=63 * 1024 * 1024

time: 62.5 us -> 62.6 us (level)
  no operation moved by 1% of the time
where the time goes in v5:
time: 62.6 us; the launch traced here: 62.3 us
  Pallas kernels  61 us (97%)
  local copies, waits for them, and re-layouts  1.38 us (2%)
    pallas_call x1, Pallas kernels, shards(): pl.pallas_call(functools.partial(kernel, bands, zs, ys, order), out_shape...  61 us
    unnamed x1, local copies, waits for them, and re-layouts  1.38 us

profile of v5, /device:TPU:1, one launch (start us, length us, event | category | flops | bytes accessed | tf_op | source)
XLA Modules:
  0.0 62.3 jit_solution(13858594142445908676)
XLA Ops:
  0.0 61.0 %encode_process.1 = bf16[32,512]{1,0:T(8,128)(2,1)} custom-call(s32[16,64]{1,0:T(8,128)} %bitcast.17, s32[1,64]{1,0:T(1,128)} %bitcast.32, bf16[256,512]{1,0:T(8,128)(2,1)} %refs_2_.1, s32[64,128]{1,0:T(8,128)} %constant.2.clone.refs_3_, s32[1,32]{1,0:T(1,128)} %bitcast.33, s32[1,512]{1,0:T(1,128)} %bitcast.18, bf16[32,512]{1,0:T(8,128)(2,1)} %refs_6_.1, ...), custom_call_target="tpu_custom_call" | custom-call | tf_op jit(solution)/shard_map/encode_process/pallas_call | solution.py:279
  61.0 1.4 %copy.30 = bf16[32,512]{1,0:T(8,128)(2,1)} copy(bf16[32,512]{1,0:T(8,128)(2,1)} %encode_process.1) | data formatting | bytes 65536
